TPU v7x, 32 devices: a whole 2x2x4 slice. The times are simulated.
32 devices in a mesh: seg: 4 (over y, core), sec: 8 (over z, x).
Axes of the slice: x: 2, y: 2, z: 4, core: 2. Of those that a mesh axis runs over, the one named last changes fastest.
Arguments:
- theta_in: float32 [4, 16, 128, 128], P('seg', 'sec'), may hold values from -6 to 6
- left_env: float32 [9, 16, 128, 128], P(None, 'sec'), may hold values from -0.0017089844 to 0.0017089844
- site_maps: float32 [4, 16, 128, 128], P('seg', 'sec'), may hold values from -1 to 2, as said below
- right_env: float32 [4, 9, 16, 128, 128], P('seg', None, 'sec'), may hold values from -8 to 8
- mpo_mask: int32 [9, 16], P(None, 'sec'), may hold values 0 or 1
- ranks: int32 [4, 16], P('seg', 'sec'), may hold values from 64 to 128
Outputs:
- theta_out: float32 [4, 16, 128, 128], P('seg', 'sec')
- density: float32 [4, 16, 128, 128], P('seg', 'sec')
Inputs may be any that keep to these rules, and one draw needn't show every extreme that they name: `site_maps`: each block of a segment's map is the identity plus a full matrix of entries of size about 1 / (4 sqrt(128)).
All inputs are finite; a program needn't handle non-finite values. No bound on the sum of `mpo_mask` on one device may be relied on, other than what follows from the above.
Results may differ from a plain program's by a relative error of at most 0.0003.
Values sent between devices are 32-bit elements; how exact they have to be, the bound alone decides.
A program may use at most 64 MiB of HBM per device.

v0:
```python
import jax
import jax.numpy as jnp
from jax import lax
from jax.sharding import PartitionSpec as P

ITERS = 4


HIGH = lax.Precision.HIGHEST
EPS = 1e-06


def from_behind(block, axis, distance):
    devices = range(lax.axis_size(axis))
    route = [(i - distance, i) for i in devices if i - distance in devices]
    return lax.ppermute(block, axis, route)


def extended(block, sides, width):
    for axis, dim in sides:
        count = lax.axis_size(axis)
        forward = [(i, i + 1) for i in range(count - 1)]
        backward = [(target, source) for source, target in forward]
        low = lax.ppermute(
            lax.slice_in_dim(block, block.shape[dim] - width, None, axis=dim), axis, forward
        )
        high = lax.ppermute(lax.slice_in_dim(block, 0, width, axis=dim), axis, backward)
        block = jnp.concatenate([low, block, high], axis=dim)
    return block


def advance_env(env, maps):
    partial_env = jnp.einsum("wkac,kcd->wkad", env, maps, precision=HIGH)
    return jnp.einsum("kab,wkad->wkbd", maps, partial_env, precision=HIGH)


def shifted_terms(padded, count, blocks):
    pieces = []
    for term in range(count):
        offset = 1 + term % 3 - 1
        pieces.append(padded[term, offset : offset + blocks])
    return jnp.stack(pieces, axis=0)


def per_device(theta_in, left_env, site_maps, right_env, mpo_mask, ranks):
    vector = theta_in[0]
    maps = site_maps[0]
    right = right_env[0]
    terms = right.shape[0]
    blocks = vector.shape[0]
    width = vector.shape[1]
    segment = lax.axis_index("seg")
    carried = left_env
    for step in range(lax.axis_size("seg") - 1):
        moved = from_behind(advance_env(carried, maps), "seg", 1)
        carried = jnp.where(segment == step + 1, moved, carried)
    weighted = carried * mpo_mask.astype(jnp.float32)[:, :, None, None]
    cells = lax.axis_size("sec") * blocks * width * width
    for step in range(ITERS):
        products = jnp.einsum("kab,wkbc->wkac", vector, right, precision=HIGH)
        padded = extended(products, (("sec", 1),), 1)
        gathered = shifted_terms(padded, terms, blocks)
        image = jnp.einsum("wkab,wkbc->kac", weighted, gathered, precision=HIGH)
        total = lax.psum(jnp.sum(image * image), "sec")
        vector = image * lax.rsqrt(total / cells + EPS)
    rows = lax.broadcasted_iota(jnp.int32, (blocks, width), 1) < ranks[0][:, None]
    trimmed = vector * rows.astype(jnp.float32)[:, :, None]
    density = jnp.einsum("kab,kcb->kac", trimmed, trimmed, precision=HIGH) / width
    return (vector[None], density[None])


def solution(mesh):
    return jax.shard_map(
        per_device,
        mesh=mesh,
        in_specs=(
            P("seg", "sec", None, None),
            P(None, "sec", None, None),
            P("seg", "sec", None, None),
            P("seg", None, "sec", None, None),
            P(None, "sec"),
            P("seg", "sec"),
        ),
        out_specs=(P("seg", "sec", None, None), P("seg", "sec", None, None)),
        check_vma=False,
    )
```

profile of v0, /device:TPU:0, one launch (start us, length us, event | category | flops | bytes accessed | tf_op | source)
XLA Modules:
  0.0 247.8 jit_solution(3775149664643838019)
XLA Ops:
  0.7 1.7 copy.8
  3.6 2.1 convolution_bitcast_fusion.8
  5.7 3.4 %collective-permute-start = (f32[9,2,128,128]{2,3,0,1:T(8,128)}, f32[9,2,128,128]{2,3,0,1:T(8,128)}, u32[]{:S(2)}, u32[]{:S(2)}) collective-permute-start(f32[9,2,128,128]{2,3,0,1:T(8,128)} %convolution_bitcast_fusion.8), channel_id=1, source_target_pairs={{0,8},{8,16},{16,24},{1,9},{9,17},{17,25},{2,10},{10,18},{18,26},{... | collective-permute-start | bytes 3538952 | tf_op jit(solution)/shard_map/ppermute | solution.py:16
  9.1 1.7 collective-permute-done
  12.2 2.2 convolution_bitcast_fusion.6
  14.4 17.5 %collective-permute-start.1 = (f32[9,2,128,128]{2,3,0,1:T(8,128)}, f32[9,2,128,128]{2,3,0,1:T(8,128)}, u32[]{:S(2)}, u32[]{:S(2)}) collective-permute-start(f32[9,2,128,128]{2,3,0,1:T(8,128)} %convolution_bitcast_fusion.6), channel_id=1, source_target_pairs={{0,8},{8,16},{16,24},{1,9},{9,17},{17,25},{2,10},{10,18},{18,26},{... | collective-permute-start | bytes 3538952 | tf_op jit(solution)/shard_map/ppermute | solution.py:16
  31.9 2.0 convolution_bitcast_fusion.3
  35.0 4.2 %collective-permute-start.3 = (f32[9,1,128,128]{2,3,0,1:T(8,128)}, f32[9,1,128,128]{2,3,0,1:T(8,128)}, u32[]{:S(2)}, u32[]{:S(2)}) collective-permute-start(f32[9,1,128,128]{2,3,0,1:T(8,128)} %get-tuple-element.9), channel_id=1, source_target_pairs={{0,1},{1,2},{2,3},{3,4},{4,5},{5,6},{6,7},{8,9},{9,10},{10,11},{11... | collective-permute-start | bytes 1769480 | tf_op jit(solution)/shard_map/ppermute | solution.py:24
  40.6 23.8 %collective-permute-done.3 = f32[9,1,128,128]{2,3,0,1:T(8,128)} collective-permute-done((f32[9,1,128,128]{2,3,0,1:T(8,128)}, f32[9,1,128,128]{2,3,0,1:T(8,128)}, u32[]{:S(2)}, u32[]{:S(2)}) %collective-permute-start.3) | collective-permute-done | bytes 589856 | tf_op jit(solution)/shard_map/ppermute | solution.py:24
  67.5 1.6 collective-permute-start.2
  73.7 2.7 %multiply_reduce_fusion.3 = (f32[]{:T(128)}, f32[2,128,128]{2,1,0:T(8,128)S(1)}) fusion(f32[9,2,128,128]{2,3,0,1:T(8,128)S(1)} %select_multiply_fusion, f32[9,2,128,128]{2,3,0,1:T(8,128)S(1)} %fusion.11), kind=kOutput, calls=%fused_computation.84 | convolution fusion | flops 453050368 | bytes 2490372 | tf_op jit(solution)/shard_map/wkab,wkbc->kac/dot_general | solution.py:63
  76.3 20.4 %psum.28 = f32[]{:T(128)} all-reduce(f32[]{:T(128)} %get-tuple-element.10), channel_id=1, replica_groups=mesh['seg'=4,'sec'=8] {'sec'}, use_global_device_ids=true, to_apply=%region_1.2 | all-reduce | flops 1 | bytes 8 | tf_op jit(solution)/shard_map/psum | solution.py:64
  101.3 21.2 %collective-permute-done.5 = f32[9,1,128,128]{3,2,0,1:T(8,128)S(1)} collective-permute-done((f32[9,1,128,128]{3,2,0,1:T(8,128)S(1)}, f32[9,1,128,128]{3,2,0,1:T(8,128)S(1)}, u32[]{:S(2)}, u32[]{:S(2)}) %collective-permute-start.5) | collective-permute-done | bytes 589856 | tf_op jit(solution)/shard_map/ppermute | solution.py:24
  122.7 2.6 %multiply_reduce_fusion.2 = (f32[]{:T(128)}, f32[2,128,128]{2,1,0:T(8,128)S(1)}) fusion(f32[9,2,128,128]{2,3,0,1:T(8,128)S(1)} %select_multiply_fusion, f32[9,2,128,128]{3,2,0,1:T(8,128)S(1)} %fusion.9), kind=kOutput, calls=%fused_computation.82 | convolution fusion | flops 453050368 | bytes 2490372 | tf_op jit(solution)/shard_map/wkab,wkbc->kac/dot_general | solution.py:63
  125.3 24.1 %psum.29 = f32[]{:T(128)} all-reduce(f32[]{:T(128)} %get-tuple-element.12), channel_id=1, replica_groups=mesh['seg'=4,'sec'=8] {'sec'}, use_global_device_ids=true, to_apply=%region_3.4 | all-reduce | flops 1 | bytes 8 | tf_op jit(solution)/shard_map/psum | solution.py:64
  151.3 1.7 collective-permute-start.7
  154.3 20.5 %collective-permute-done.7 = f32[9,1,128,128]{3,2,0,1:T(8,128)S(1)} collective-permute-done((f32[9,1,128,128]{3,2,0,1:T(8,128)S(1)}, f32[9,1,128,128]{3,2,0,1:T(8,128)S(1)}, u32[]{:S(2)}, u32[]{:S(2)}) %collective-permute-start.7) | collective-permute-done | bytes 589856 | tf_op jit(solution)/shard_map/ppermute | solution.py:24
  175.0 2.6 %multiply_reduce_fusion.1 = (f32[]{:T(128)}, f32[2,128,128]{2,1,0:T(8,128)S(1)}) fusion(f32[9,2,128,128]{2,3,0,1:T(8,128)S(1)} %select_multiply_fusion, f32[9,2,128,128]{3,2,0,1:T(8,128)S(1)} %fusion.7), kind=kOutput, calls=%fused_computation.80 | convolution fusion | flops 453050368 | bytes 2490372 | tf_op jit(solution)/shard_map/wkab,wkbc->kac/dot_general | solution.py:63
  177.6 20.2 %psum.30 = f32[]{:T(128)} all-reduce(f32[]{:T(128)} %get-tuple-element.14), channel_id=1, replica_groups=mesh['seg'=4,'sec'=8] {'sec'}, use_global_device_ids=true, to_apply=%region_5.6 | all-reduce | flops 1 | bytes 8 | tf_op jit(solution)/shard_map/psum | solution.py:64
  199.7 1.5 collective-permute-start.9
  201.2 1.5 collective-permute-start.10
  202.8 19.5 %collective-permute-done.9 = f32[9,1,128,128]{3,2,0,1:T(8,128)S(1)} collective-permute-done((f32[9,1,128,128]{3,2,0,1:T(8,128)S(1)}, f32[9,1,128,128]{3,2,0,1:T(8,128)S(1)}, u32[]{:S(2)}, u32[]{:S(2)}) %collective-permute-start.9) | collective-permute-done | bytes 589856 | tf_op jit(solution)/shard_map/ppermute | solution.py:24
  222.5 2.6 %multiply_reduce_fusion = (f32[]{:T(128)}, f32[2,128,128]{2,1,0:T(8,128)S(1)}) fusion(f32[9,2,128,128]{2,3,0,1:T(8,128)S(1)} %select_multiply_fusion, f32[9,2,128,128]{3,2,0,1:T(8,128)S(1)} %fusion.5), kind=kOutput, calls=%fused_computation.78 | convolution fusion | flops 453050368 | bytes 2490372 | tf_op jit(solution)/shard_map/wkab,wkbc->kac/dot_general | solution.py:63
  225.1 20.2 %psum.31 = f32[]{:T(128)} all-reduce(f32[]{:T(128)} %get-tuple-element.16), channel_id=1, replica_groups=mesh['seg'=4,'sec'=8] {'sec'}, use_global_device_ids=true, to_apply=%region_7.8 | all-reduce | flops 1 | bytes 8 | tf_op jit(solution)/shard_map/psum | solution.py:64
  (77 shorter events, 22.3 us)
Async XLA Ops:
  0.6 31.2 %copy-start = (f32[1,9,2,128,128]{4,3,2,1,0:T(8,128)S(1)}, f32[1,9,2,128,128]{4,3,2,1,0:T(8,128)}, u32[]{:S(2)}) copy-start(f32[1,9,2,128,128]{4,3,2,1,0:T(8,128)} %param.9) | copy-start | bytes 3538948
  0.6 1.8 copy-start.1
  5.7 5.2 %collective-permute-start = (f32[9,2,128,128]{2,3,0,1:T(8,128)}, f32[9,2,128,128]{2,3,0,1:T(8,128)}, u32[]{:S(2)}, u32[]{:S(2)}) collective-permute-start(f32[9,2,128,128]{2,3,0,1:T(8,128)} %convolution_bitcast_fusion.8), channel_id=1, source_target_pairs={{0,8},{8,16},{16,24},{1,9},{9,17},{17,25},{2,10},{10,18},{18,26},{... | collective-permute-start | bytes 3538952 | tf_op jit(solution)/shard_map/ppermute | solution.py:16
  9.1 1.9 copy-start.2
  12.2 19.7 %copy-start.4 = (f32[1,2,128,128]{3,2,1,0:T(8,128)S(1)}, f32[1,2,128,128]{3,2,1,0:T(8,128)}, u32[]{:S(2)}) copy-start(f32[1,2,128,128]{3,2,1,0:T(8,128)} %param.6) | copy-start | bytes 393220
  14.4 50.8 %collective-permute-start.1 = (f32[9,2,128,128]{2,3,0,1:T(8,128)}, f32[9,2,128,128]{2,3,0,1:T(8,128)}, u32[]{:S(2)}, u32[]{:S(2)}) collective-permute-start(f32[9,2,128,128]{2,3,0,1:T(8,128)} %convolution_bitcast_fusion.6), channel_id=1, source_target_pairs={{0,8},{8,16},{16,24},{1,9},{9,17},{17,25},{2,10},{10,18},{18,26},{... | collective-permute-start | bytes 3538952 | tf_op jit(solution)/shard_map/ppermute | solution.py:16
  33.9 6.6 %copy-start.5 = (s32[9,2]{0,1:T(2,128)S(1)}, s32[9,2]{0,1:T(2,128)}, u32[]{:S(2)}) copy-start(s32[9,2]{0,1:T(2,128)} %param.10) | copy-start | bytes 220
  35.0 29.3 %collective-permute-start.3 = (f32[9,1,128,128]{2,3,0,1:T(8,128)}, f32[9,1,128,128]{2,3,0,1:T(8,128)}, u32[]{:S(2)}, u32[]{:S(2)}) collective-permute-start(f32[9,1,128,128]{2,3,0,1:T(8,128)} %get-tuple-element.9), channel_id=1, source_target_pairs={{0,1},{1,2},{2,3},{3,4},{4,5},{5,6},{6,7},{8,9},{9,10},{10,11},{11... | collective-permute-start | bytes 1769480 | tf_op jit(solution)/shard_map/ppermute | solution.py:24
  39.2 29.9 %collective-permute-start.4 = (f32[9,1,128,128]{2,3,0,1:T(8,128)}, f32[9,1,128,128]{2,3,0,1:T(8,128)}, u32[]{:S(2)}, u32[]{:S(2)}) collective-permute-start(f32[9,1,128,128]{2,3,0,1:T(8,128)} %get-tuple-element.8), channel_id=1, source_target_pairs={{1,0},{2,1},{3,2},{4,3},{5,4},{6,5},{7,6},{9,8},{10,9},{11,10},{12... | collective-permute-start | bytes 1769480 | tf_op jit(solution)/shard_map/ppermute | solution.py:27
  40.5 24.6 %copy-start.3 = (f32[1,2,128,128]{3,2,1,0:T(8,128)S(1)}, f32[1,2,128,128]{3,2,1,0:T(8,128)}, u32[]{:S(2)}) copy-start(f32[1,2,128,128]{3,2,1,0:T(8,128)} %param.8) | copy-start | bytes 393220
  67.5 5.9 %collective-permute-start.2 = (f32[9,2,128,128]{2,3,0,1:T(8,128)S(1)}, f32[9,2,128,128]{2,3,0,1:T(8,128)S(1)}, u32[]{:S(2)}, u32[]{:S(2)}) collective-permute-start(f32[9,2,128,128]{2,3,0,1:T(8,128)S(1)} %convolution_bitcast_fusion.4), channel_id=1, source_target_pairs={{0,8},{8,16},{16,24},{1,9},{9,17},{17,25},{2,10},{10,18},{18,26},{... | collective-permute-start | bytes 3538952 | tf_op jit(solution)/shard_map/ppermute | solution.py:16
  98.7 23.8 %collective-permute-start.5 = (f32[9,1,128,128]{3,2,0,1:T(8,128)S(1)}, f32[9,1,128,128]{3,2,0,1:T(8,128)S(1)}, u32[]{:S(2)}, u32[]{:S(2)}) collective-permute-start(f32[9,1,128,128]{3,2,0,1:T(8,128)S(1)} %get-tuple-element.7), channel_id=1, source_target_pairs={{0,1},{1,2},{2,3},{3,4},{4,5},{5,6},{6,7},{8,9},{9,10},{10,11},{11... | collective-permute-start | bytes 1769480 | tf_op jit(solution)/shard_map/ppermute | solution.py:24
  100.0 22.5 %collective-permute-start.6 = (f32[9,1,128,128]{3,2,0,1:T(8,128)S(1)}, f32[9,1,128,128]{3,2,0,1:T(8,128)S(1)}, u32[]{:S(2)}, u32[]{:S(2)}) collective-permute-start(f32[9,1,128,128]{3,2,0,1:T(8,128)S(1)} %get-tuple-element.6), channel_id=1, source_target_pairs={{1,0},{2,1},{3,2},{4,3},{5,4},{6,5},{7,6},{9,8},{10,9},{11,10},{12... | collective-permute-start | bytes 1769480 | tf_op jit(solution)/shard_map/ppermute | solution.py:27
  151.3 23.5 %collective-permute-start.7 = (f32[9,1,128,128]{3,2,0,1:T(8,128)S(1)}, f32[9,1,128,128]{3,2,0,1:T(8,128)S(1)}, u32[]{:S(2)}, u32[]{:S(2)}) collective-permute-start(f32[9,1,128,128]{3,2,0,1:T(8,128)S(1)} %get-tuple-element.5), channel_id=1, source_target_pairs={{0,1},{1,2},{2,3},{3,4},{4,5},{5,6},{6,7},{8,9},{9,10},{10,11},{11... | collective-permute-start | bytes 1769480 | tf_op jit(solution)/shard_map/ppermute | solution.py:24
  153.0 21.8 %collective-permute-start.8 = (f32[9,1,128,128]{3,2,0,1:T(8,128)S(1)}, f32[9,1,128,128]{3,2,0,1:T(8,128)S(1)}, u32[]{:S(2)}, u32[]{:S(2)}) collective-permute-start(f32[9,1,128,128]{3,2,0,1:T(8,128)S(1)} %get-tuple-element.4), channel_id=1, source_target_pairs={{1,0},{2,1},{3,2},{4,3},{5,4},{6,5},{7,6},{9,8},{10,9},{11,10},{12... | collective-permute-start | bytes 1769480 | tf_op jit(solution)/shard_map/ppermute | solution.py:27
  199.6 3.1 %copy-start.6 = (s32[1,2]{1,0:T(1,128)S(1)}, s32[1,2]{1,0:T(1,128)}, u32[]{:S(2)}) copy-start(s32[1,2]{1,0:T(1,128)} %param.11) | copy-start | bytes 28
  199.7 22.6 %collective-permute-start.9 = (f32[9,1,128,128]{3,2,0,1:T(8,128)S(1)}, f32[9,1,128,128]{3,2,0,1:T(8,128)S(1)}, u32[]{:S(2)}, u32[]{:S(2)}) collective-permute-start(f32[9,1,128,128]{3,2,0,1:T(8,128)S(1)} %get-tuple-element.3), channel_id=1, source_target_pairs={{0,1},{1,2},{2,3},{3,4},{4,5},{5,6},{6,7},{8,9},{9,10},{10,11},{11... | collective-permute-start | bytes 1769480 | tf_op jit(solution)/shard_map/ppermute | solution.py:24
  201.2 21.1 %collective-permute-start.10 = (f32[9,1,128,128]{3,2,0,1:T(8,128)S(1)}, f32[9,1,128,128]{3,2,0,1:T(8,128)S(1)}, u32[]{:S(2)}, u32[]{:S(2)}) collective-permute-start(f32[9,1,128,128]{3,2,0,1:T(8,128)S(1)} %get-tuple-element.2), channel_id=1, source_target_pairs={{1,0},{2,1},{3,2},{4,3},{5,4},{6,5},{7,6},{9,8},{10,9},{11,10},{12... | collective-permute-start | bytes 1769480 | tf_op jit(solution)/shard_map/ppermute | solution.py:27
where the time goes:
time: 251 us; the launch traced here: 248 us
  waiting for transfers between devices  86.6 us (35%)
  blocking collectives  85 us (34%)
  starting transfers between devices  36.5 us (15%)
  matrix products  25.9 us (10%)
  other arithmetic  6.4 us (3%)
  between operations  3.97 us (2%)
  local copies, waits for them, and re-layouts  3.33 us (1%)
    psum x4, blocking collectives, per_device(): total = lax.psum(jnp.sum(image * image), 'sec')  85 us
    ppermute x4, waiting for transfers between devices, extended(): lax.ppermute(lax.slice_in_dim(block, block.shape[dim] - width, None, axis...  84.9 us
    ppermute x3, starting transfers between devices, from_behind(): return lax.ppermute(block, axis, route)  22.4 us
    dot_general x4, matrix products, per_device(): image = jnp.einsum('wkab,wkbc->kac', weighted, gathered, precision=HIGH)  10.5 us
    ppermute x4, starting transfers between devices, extended(): lax.ppermute(lax.slice_in_dim(block, block.shape[dim] - width, None, axis...  8.73 us
    dot_general x3, matrix products, advance_env(): return jnp.einsum('kab,wkad->wkbd', maps, partial_env, precision=HIGH)  5.43 us
    ppermute x4, starting transfers between devices, extended(): lax.ppermute(lax.slice_in_dim(block, 0, width, axis=dim), axis, backward)  5.38 us
    dot_general x4, matrix products, per_device(): products = jnp.einsum('kab,wkbc->wkac', vector, right, precision=HIGH)  5.31 us
  transfers between devices with their start and end apart: 11, of which 5 were waited for; matrix products, arithmetic and copies ran while one was open for 4% of the time, Pallas kernels for 0%

commit v1 on v0

v1 whole, which is shorter than its diff:
```python
import functools

import jax
import jax.numpy as jnp
from jax import lax
from jax.experimental import pallas as pl
from jax.experimental.pallas import tpu as pltpu
from jax.sharding import PartitionSpec as P

ITERS = 4
EPS = 1e-06
MESH = pl.DeviceIdType.MESH
F32, BF16 = jnp.float32, jnp.bfloat16


def split(x):
    high = x.astype(BF16)
    low = (x - high.astype(F32)).astype(BF16)
    return high, low


def wide(x):
    return jnp.concatenate(split(x), axis=1)


def twice(x):
    pair = wide(x)
    return jnp.concatenate([pair, pair], axis=0)


def dot(a, b):
    return lax.dot_general(a, b, (((1,), (0,)), ((), ())), preferred_element_type=F32)


def halves(x):
    n = x.shape[1] // 2
    return x[:, :n] + x[:, n:]


def squares(x):
    return jnp.sum((x * x).reshape(-1, 8, x.shape[1]), axis=0)


def kernel(
    n_seg, n_sec, groups, theta, left, maps, right, mask, ranks, theta_out, density,
    lf, rt, mp, amat, rhalo, vh, vs, l2, r2, red,
    local_sem, m_send, m_recv, r_send, r_recv, v_send, v_recv, s_send, s_recv,
):
    seg, sec = lax.axis_index("seg"), lax.axis_index("sec")
    blocks, n = theta.shape[1], theta.shape[2]
    terms = left.shape[0]
    has_low, has_high = sec > 0, sec < n_sec - 1
    row = {}
    start = {}
    for d in (-1, 0, 1):
        start[d] = len(row) * n
        for w in groups[d]:
            row[w] = len(row) * n

    loads = [
        pltpu.make_async_copy(left, lf, local_sem.at[0]),
        pltpu.make_async_copy(right.at[0], rt, local_sem.at[1]),
        pltpu.make_async_copy(theta.at[0], vs.at[0], local_sem.at[2]),
    ]
    for load in loads:
        load.start()

    barrier = pltpu.get_barrier_semaphore()
    for d in range(1, n_seg):
        pl.semaphore_signal(barrier, inc=1, device_id={"seg": lax.rem(seg + d, n_seg)}, device_id_type=MESH)
    for d in range(1, n_sec):
        pl.semaphore_signal(barrier, inc=1, device_id={"sec": lax.rem(sec + d, n_sec)}, device_id_type=MESH)
    pl.semaphore_wait(barrier, n_seg + n_sec - 2)

    def m_copy(d):
        return pltpu.make_async_remote_copy(
            src_ref=maps.at[0], dst_ref=mp.at[seg], send_sem=m_send.at[d - 1], recv_sem=m_recv.at[seg],
            device_id={"seg": seg + d}, device_id_type=MESH,
        )

    def m_arrival(j):
        return pltpu.make_async_remote_copy(
            src_ref=maps.at[0], dst_ref=mp.at[j], send_sem=m_send.at[0], recv_sem=m_recv.at[j],
            device_id={"seg": j}, device_id_type=MESH,
        )

    def v_copy(t, source, side):
        other = sec - 1 if side == 0 else sec + 1
        return pltpu.make_async_remote_copy(
            src_ref=source, dst_ref=vh.at[t, 1 - side], send_sem=v_send.at[t, side],
            recv_sem=v_recv.at[t, 1 - side], device_id={"sec": other}, device_id_type=MESH,
        )

    def v_arrival(t, side):
        other = sec - 1 if side == 0 else sec + 1
        return pltpu.make_async_remote_copy(
            src_ref=vs.at[0, 0], dst_ref=vh.at[t, side], send_sem=v_send.at[t, side],
            recv_sem=v_recv.at[t, side], device_id={"sec": other}, device_id_type=MESH,
        )

    def r_copies(side):
        other = sec - 1 if side == 0 else sec + 1
        q, shift = (0, 1) if side == 0 else (blocks - 1, -1)
        return [
            pltpu.make_async_remote_copy(
                src_ref=right.at[0, w, q], dst_ref=rhalo.at[1 - side, i], send_sem=r_send.at[side, i],
                recv_sem=r_recv.at[1 - side, i], device_id={"sec": other}, device_id_type=MESH,
            )
            for i, w in enumerate(groups[shift])
        ]

    def r_arrivals(side):
        other = sec - 1 if side == 0 else sec + 1
        shift = -1 if side == 0 else 1
        return [
            pltpu.make_async_remote_copy(
                src_ref=right.at[0, w, 0], dst_ref=rhalo.at[side, i], send_sem=r_send.at[side, i],
                recv_sem=r_recv.at[side, i], device_id={"sec": other}, device_id_type=MESH,
            )
            for i, w in enumerate(groups[shift])
        ]

    def s_copy(stage, d):
        return pltpu.make_async_remote_copy(
            src_ref=red.at[stage, sec], dst_ref=red.at[stage, sec], send_sem=s_send.at[stage, d],
            recv_sem=s_recv.at[stage, sec], device_id={"sec": lax.rem(sec + d, n_sec)}, device_id_type=MESH,
        )

    def s_arrival(stage, d):
        other = lax.rem(sec + d, n_sec)
        return pltpu.make_async_remote_copy(
            src_ref=red.at[stage, sec], dst_ref=red.at[stage, other], send_sem=s_send.at[stage, d],
            recv_sem=s_recv.at[stage, other], device_id={"sec": other}, device_id_type=MESH,
        )

    for d in range(1, n_seg):
        @pl.when(seg + d < n_seg)
        def _():
            m_copy(d).start()

    for side, there in ((0, has_low), (1, has_high)):
        q = 0 if side == 0 else blocks - 1
        @pl.when(there)
        def _():
            v_copy(0, theta.at[0, q], side).start()
            for copy in r_copies(side):
                copy.start()

        @pl.when(jnp.logical_not(there))
        def _():
            rhalo[side] = jnp.zeros_like(rhalo[side])
            for t in range(ITERS):
                vh[t, side] = jnp.zeros_like(vh[t, side])

    loads[0].wait()
    for q in range(blocks):
        for w in range(terms):
            l2[q, row[w] : row[w] + n, :] = wide(lf[w, q] * mask[w, q].astype(F32))
    loads[1].wait()
    for q in range(blocks):
        for d in (-1, 0, 1):
            if 0 <= q + d < blocks:
                for w in groups[d]:
                    r2[q, row[w] : row[w] + n, :] = wide(rt[w, q + d])
    loads[2].wait()

    @pl.when(seg == 0)
    def _():
        here = lax.broadcasted_iota(jnp.int32, (n, n), 0)
        across = lax.broadcasted_iota(jnp.int32, (n, n), 1)
        for q in range(blocks):
            amat[q] = (here == across).astype(F32)

    for j in range(n_seg - 1):
        @pl.when(j < seg)
        def _():
            m_arrival(j).wait_recv()
            for q in range(blocks):
                if j == 0:
                    amat[q] = mp[0, q]
                else:
                    amat[q] = halves(dot(wide(amat[q]), twice(mp[j, q])))

    for q in range(blocks):
        a = amat[q]
        turned = wide(a.T)
        doubled = twice(a)
        for d in (-1, 0, 1):
            for w in groups[d]:
                part = halves(dot(l2[q, row[w] : row[w] + n, :], doubled))
                l2[q, row[w] : row[w] + n, :] = wide(halves(dot(turned, twice(part))))

    def contribution(q, d, vector2):
        size = len(groups[d]) * n
        x = halves(dot(l2[q, start[d] : start[d] + size, :], vector2))
        x = jnp.concatenate([x[i * n : (i + 1) * n] for i in range(len(groups[d]))], axis=1)
        x = jnp.concatenate(split(x), axis=0)
        y = halves(dot(x, r2[q, start[d] : start[d] + size, :]))
        return y[:n] + y[n:]

    def step(t, _):
        own = [twice(vs[t, q]) for q in range(blocks)]
        image = []
        for q in range(blocks):
            total = None
            for d in (-1, 0, 1):
                if 0 <= q + d < blocks:
                    y = contribution(q, d, own[q + d])
                    total = y if total is None else total + y
            vs[t + 1, q] = total

        tile = jnp.zeros((8, n), F32)
        for side, there in ((0, has_low), (1, has_high)):
            q, d = (0, -1) if side == 0 else (blocks - 1, 1)

            @pl.when(there & (t == 0))
            def _():
                for copy in r_arrivals(side):
                    copy.wait_recv()

            @pl.when(t == 0)
            def _():
                for i, w in enumerate(groups[d]):
                    r2[q, row[w] : row[w] + n, :] = wide(rhalo[side, i])

            @pl.when(there)
            def _():
                v_arrival(t, side).wait_recv()

            vs[t + 1, q] = vs[t + 1, q] + contribution(q, d, twice(vh[t, side]))
            if blocks > 1:
                @pl.when(there & (t < ITERS - 1))
                def _():
                    v_copy(t + 1, vs.at[t + 1, q], side).start()

        if blocks == 1:
            for side, there in ((0, has_low), (1, has_high)):
                @pl.when(there & (t < ITERS - 1))
                def _():
                    v_copy(t + 1, vs.at[t + 1, 0], side).start()

        @pl.when(t < ITERS - 1)
        def _():
            total = squares(vs[t + 1, 0])
            for q in range(1, blocks):
                total = total + squares(vs[t + 1, q])
            red[t // 2, sec, t % 2] = total

        @pl.when(t == 1)
        def _():
            for d in range(1, n_sec):
                s_copy(0, d).start()

        return 0

    lax.fori_loop(0, ITERS, step, 0)

    cells = n_sec * blocks * n * n

    def whole(stage):
        total = red[stage, 0]
        for other in range(1, n_sec):
            total = total + red[stage, other]
        first = jnp.sum(total[0], keepdims=True)
        second = jnp.sum(total[1], keepdims=True)
        return first / cells, second / cells

    for d in range(1, n_sec):
        s_arrival(0, d).wait_recv()
    m1, m2 = whole(0)
    s1 = lax.rsqrt(m1 + EPS)
    s12 = s1 * lax.rsqrt(s1 * s1 * m2 + EPS)
    last = [vs[ITERS, q] * s12 for q in range(blocks)]
    total = squares(last[0])
    for q in range(1, blocks):
        total = total + squares(last[q])
    red[1, sec, 1] = total
    for d in range(1, n_sec):
        s_copy(1, d).start()

    here = lax.broadcasted_iota(jnp.int32, (n, n), 0)
    across = lax.broadcasted_iota(jnp.int32, (n, n), 1)
    for q in range(blocks):
        theta_out[0, q] = last[q]
        kept = ((here < ranks[0, q]) & (across < ranks[0, q])).astype(F32)
        density[0, q] = halves(dot(wide(last[q]), twice(last[q].T))) * kept

    for d in range(1, n_sec):
        s_arrival(1, d).wait_recv()
    m3, m4 = whole(1)
    s3 = lax.rsqrt(s12 * s12 * m3 + EPS)
    s34 = s3 * lax.rsqrt(s3 * s3 * m4 + EPS)
    for q in range(blocks):
        theta_out[0, q] = theta_out[0, q] * s34
        density[0, q] = density[0, q] * (s34 * s34 / n)

    for d in range(1, n_seg):
        @pl.when(seg + d < n_seg)
        def _():
            m_copy(d).wait_send()
    for side, there in ((0, has_low), (1, has_high)):
        q = 0 if side == 0 else blocks - 1
        @pl.when(there)
        def _():
            v_copy(0, theta.at[0, q], side).wait_send()
            for t in range(1, ITERS):
                v_copy(t, vs.at[t, q], side).wait_send()
            for copy in r_copies(side):
                copy.wait_send()
    for stage in range(2):
        for d in range(1, n_sec):
            s_copy(stage, d).wait_send()


def per_device(n_seg, n_sec, theta_in, left_env, site_maps, right_env, mpo_mask, ranks):
    terms, blocks, n, _ = left_env.shape
    groups = {d: [w for w in range(terms) if w % 3 - 1 == d] for d in (-1, 0, 1)}
    most = max(len(g) for g in groups.values())
    block = (n, n)
    anywhere = pl.BlockSpec(memory_space=pl.ANY)
    scalars = pl.BlockSpec(memory_space=pltpu.SMEM)
    vmem = pl.BlockSpec(memory_space=pltpu.VMEM)
    out = jax.ShapeDtypeStruct(theta_in.shape, F32)
    dma = pltpu.SemaphoreType.DMA
    return pl.pallas_call(
        functools.partial(kernel, n_seg, n_sec, groups),
        out_shape=(out, out),
        in_specs=[anywhere, anywhere, anywhere, anywhere, scalars, scalars],
        out_specs=(vmem, vmem),
        scratch_shapes=[
            pltpu.VMEM((terms, blocks) + block, F32),
            pltpu.VMEM((terms, blocks) + block, F32),
            pltpu.VMEM((n_seg, blocks) + block, F32),
            pltpu.VMEM((blocks,) + block, F32),
            pltpu.VMEM((2, most) + block, F32),
            pltpu.VMEM((ITERS, 2) + block, F32),
            pltpu.VMEM((ITERS + 1, blocks) + block, F32),
            pltpu.VMEM((blocks, terms * n, 2 * n), BF16),
            pltpu.VMEM((blocks, terms * n, 2 * n), BF16),
            pltpu.VMEM((2, n_sec, 2, 8, n), F32),
            dma((3,)),
            dma((n_seg,)),
            dma((n_seg,)),
            dma((2, most)),
            dma((2, most)),
            dma((ITERS, 2)),
            dma((ITERS, 2)),
            dma((2, n_sec)),
            dma((2, n_sec)),
        ],
        compiler_params=pltpu.CompilerParams(
            collective_id=0, has_side_effects=True, vmem_limit_bytes=48 * 1024 * 1024
        ),
        cost_estimate=pl.CostEstimate(flops=2 * n**3 * 4 * 200, bytes_accessed=4 * n * n * 60, transcendentals=0),
    )(theta_in, left_env, site_maps, right_env, mpo_mask, ranks)


def solution(mesh):
    n_seg, n_sec = mesh.shape["seg"], mesh.shape["sec"]
    return jax.shard_map(
        functools.partial(per_device, n_seg, n_sec),
        mesh=mesh,
        in_specs=(
            P("seg", "sec", None, None),
            P(None, "sec", None, None),
            P("seg", "sec", None, None),
            P("seg", None, "sec", None, None),
            P(None, "sec"),
            P("seg", "sec"),
        ),
        out_specs=(P("seg", "sec", None, None), P("seg", "sec", None, None)),
        check_vma=False,
    )
```

time: 251 us -> 50.6 us (0.20); the launches traced: 248 us -> 50.4 us
  waiting for transfers between devices: 86.6 us -> 0 us
  blocking collectives: 85 us -> 0 us
  Pallas kernels: 0 us -> 42.7 us
  starting transfers between devices: 36.5 us -> 0 us
  matrix products: 25.9 us -> 0 us
  other arithmetic: 6.4 us -> 0 us
  local copies, waits for them, and re-layouts: 3.33 us -> 7.08 us
  between operations: 3.97 us -> 0.64 us
    ppermute x11 -> x0, waiting for transfers between devices: 86.6 us -> none  [the longest x4 84.9 us: extended(): lax.ppermute(lax.slice_in_dim(block, block.shape[dim] - width, None, axis...]
    psum x4 -> x0, blocking collectives: 85 us -> none  [per_device(): total = lax.psum(jnp.sum(image * image), 'sec')]
    pallas_call x0 -> x1, Pallas kernels: none -> 42.7 us  [per_device(): pl.pallas_call(functools.partial(kernel, n_seg, n_sec, groups), out_shape...]
    ppermute x11 -> x0, starting transfers between devices: 36.5 us -> none  [the longest x3 22.4 us: from_behind(): return lax.ppermute(block, axis, route)]
    dot_general x15 -> x0, matrix products: 25.9 us -> none  [the longest x4 10.5 us: per_device(): image = jnp.einsum('wkab,wkbc->kac', weighted, gathered, precision=HIGH)]
    unnamed x27 -> x13, local copies, waits for them, and re-layouts: 1.93 us -> 7.08 us
    unnamed x20 -> x0, other arithmetic: 4.42 us -> none
  transfers between devices with their start and end apart: 11 -> 0, of which waited for: 5 -> 0; matrix products, arithmetic and copies ran while one was open for 4% -> 0% of each run, Pallas kernels for 0% -> 0%
where the time goes in v1:
time: 50.6 us; the launch traced here: 50.4 us
  Pallas kernels  42.7 us (84%)
  local copies, waits for them, and re-layouts  7.08 us (14%)
  between operations  0.64 us (1%)
    pallas_call x1, Pallas kernels, per_device(): pl.pallas_call(functools.partial(kernel, n_seg, n_sec, groups), out_shape...  42.7 us
    unnamed x13, local copies, waits for them, and re-layouts  7.08 us

profile of v1, /device:TPU:0, one launch (start us, length us, event | category | flops | bytes accessed | tf_op | source)
XLA Modules:
  0.0 50.4 jit_solution(5448358900805170018)
XLA Ops:
  0.6 0.8 %copy.8.mask = s32[9,2]{1,0:T(8,128)S(1)} copy(s32[9,2]{0,1:T(2,128)} %param.10) | data formatting | bytes 144 | tf_op args[4]
  1.4 0.0 copy-start
  1.4 1.3 %copy-done = f32[9,2,128,128]{3,2,1,0:T(8,128)S(1)} copy-done((f32[9,2,128,128]{3,2,1,0:T(8,128)S(1)}, f32[9,2,128,128]{3,2,1,0:T(8,128)}, u32[]{:S(2)}) %copy-start) | copy-done | bytes 1179672
  2.7 0.0 copy-start.1
  2.7 1.3 %copy-done.1 = f32[1,9,2,128,128]{4,3,2,1,0:T(8,128)S(1)} copy-done((f32[1,9,2,128,128]{4,3,2,1,0:T(8,128)S(1)}, f32[1,9,2,128,128]{4,3,2,1,0:T(8,128)}, u32[]{:S(2)}) %copy-start.1) | copy-done | bytes 1179672
  3.9 0.0 copy-start.2
  3.9 0.9 %copy-done.2 = f32[1,2,128,128]{3,2,1,0:T(8,128)S(1)} copy-done((f32[1,2,128,128]{3,2,1,0:T(8,128)S(1)}, f32[1,2,128,128]{3,2,1,0:T(8,128)}, u32[]{:S(2)}) %copy-start.2) | copy-done | bytes 131096
  4.8 0.0 copy-start.3
  4.8 0.9 %copy-done.3 = f32[1,2,128,128]{3,2,1,0:T(8,128)S(1)} copy-done((f32[1,2,128,128]{3,2,1,0:T(8,128)S(1)}, f32[1,2,128,128]{3,2,1,0:T(8,128)}, u32[]{:S(2)}) %copy-start.3) | copy-done | bytes 131096
  5.7 0.0 copy-start.4
  5.8 0.7 %copy-done.4 = s32[1,2]{1,0:T(1,128)S(1)} copy-done((s32[1,2]{1,0:T(1,128)S(1)}, s32[1,2]{1,0:T(1,128)}, u32[]{:S(2)}) %copy-start.4) | copy-done | bytes 32
  6.4 42.7 %shard_map.77 = (f32[1,2,128,128]{3,2,1,0:T(8,128)S(1)}, f32[1,2,128,128]{3,2,1,0:T(8,128)S(1)}) custom-call(f32[1,2,128,128]{3,2,1,0:T(8,128)S(1)} %copy-done.2, f32[9,2,128,128]{3,2,1,0:T(8,128)S(1)} %copy-done, f32[1,2,128,128]{3,2,1,0:T(8,128)S(1)} %copy-done.3, f32[1,9,2,128,128]{4,3,2,1,0:T(8,128)S(1)} %copy-done.1, s32[9,2]{1,0:T(8,128)S(1)} %copy.8.mask, ...), custom_call_target="tpu_custom_call" | custom-call | flops 3355443200 | bytes 3932160 | tf_op jit(solution)/shard_map/pallas_call | solution.py:325
  49.1 0.7 %copy.11 = f32[1,2,128,128]{3,2,1,0:T(8,128)} copy(f32[1,2,128,128]{3,2,1,0:T(8,128)S(1)} %get-tuple-element.4) | data formatting | bytes 262144
  49.7 0.7 %copy.12 = f32[1,2,128,128]{3,2,1,0:T(8,128)} copy(f32[1,2,128,128]{3,2,1,0:T(8,128)S(1)} %get-tuple-element.5) | data formatting | bytes 262144
Async XLA Ops:
  1.4 1.3 %copy-start = (f32[9,2,128,128]{3,2,1,0:T(8,128)S(1)}, f32[9,2,128,128]{3,2,1,0:T(8,128)}, u32[]{:S(2)}) copy-start(f32[9,2,128,128]{3,2,1,0:T(8,128)} %left.1) | copy-start | bytes 3538948
  2.7 1.3 %copy-start.1 = (f32[1,9,2,128,128]{4,3,2,1,0:T(8,128)S(1)}, f32[1,9,2,128,128]{4,3,2,1,0:T(8,128)}, u32[]{:S(2)}) copy-start(f32[1,9,2,128,128]{4,3,2,1,0:T(8,128)} %right.1) | copy-start | bytes 3538948
  3.9 0.9 %copy-start.2 = (f32[1,2,128,128]{3,2,1,0:T(8,128)S(1)}, f32[1,2,128,128]{3,2,1,0:T(8,128)}, u32[]{:S(2)}) copy-start(f32[1,2,128,128]{3,2,1,0:T(8,128)} %theta.1) | copy-start | bytes 393220
  4.8 0.9 %copy-start.3 = (f32[1,2,128,128]{3,2,1,0:T(8,128)S(1)}, f32[1,2,128,128]{3,2,1,0:T(8,128)}, u32[]{:S(2)}) copy-start(f32[1,2,128,128]{3,2,1,0:T(8,128)} %maps.1) | copy-start | bytes 393220
  5.7 0.7 %copy-start.4 = (s32[1,2]{1,0:T(1,128)S(1)}, s32[1,2]{1,0:T(1,128)}, u32[]{:S(2)}) copy-start(s32[1,2]{1,0:T(1,128)} %ranks.1) | copy-start | bytes 28

commit v2 on v1

--- a/solution.py
+++ b/solution.py
@@ -155,7 +155,7 @@
     loads[0].wait()
     for q in range(blocks):
         for w in range(terms):
-            l2[q, row[w] : row[w] + n, :] = wide(lf[w, q] * mask[w, q].astype(F32))
+            l2[q, row[w] : row[w] + n, :] = wide(lf[w, q] * mask[q, w].astype(F32))
     loads[1].wait()
     for q in range(blocks):
         for d in (-1, 0, 1):
@@ -209,35 +209,32 @@
                     total = y if total is None else total + y
             vs[t + 1, q] = total
 
-        tile = jnp.zeros((8, n), F32)
-        for side, there in ((0, has_low), (1, has_high)):
-            q, d = (0, -1) if side == 0 else (blocks - 1, 1)
-
-            @pl.when(there & (t == 0))
-            def _():
-                for copy in r_arrivals(side):
-                    copy.wait_recv()
-
-            @pl.when(t == 0)
-            def _():
+        sides = ((0, has_low, 0, -1), (1, has_high, blocks - 1, 1))
+
+        @pl.when(t == 0)
+        def _():
+            for side, there, q, d in sides:
+                @pl.when(there)
+                def _():
+                    for copy in r_arrivals(side):
+                        copy.wait_recv()
+
+            for side, there, q, d in sides:
                 for i, w in enumerate(groups[d]):
                     r2[q, row[w] : row[w] + n, :] = wide(rhalo[side, i])
 
+        for side, there, q, d in sides:
             @pl.when(there)
             def _():
                 v_arrival(t, side).wait_recv()
 
-            vs[t + 1, q] = vs[t + 1, q] + contribution(q, d, twice(vh[t, side]))
-            if blocks > 1:
-                @pl.when(there & (t < ITERS - 1))
-                def _():
-                    v_copy(t + 1, vs.at[t + 1, q], side).start()
-
-        if blocks == 1:
-            for side, there in ((0, has_low), (1, has_high)):
-                @pl.when(there & (t < ITERS - 1))
-                def _():
-                    v_copy(t + 1, vs.at[t + 1, 0], side).start()
+        crossed = [contribution(q, d, twice(vh[t, side])) for side, _, q, d in sides]
+        for side, there, q, d in sides:
+            vs[t + 1, q] = vs[t + 1, q] + crossed[side]
+        for side, there, q, d in sides:
+            @pl.when(there & (t < ITERS - 1))
+            def _():
+                v_copy(t + 1, vs.at[t + 1, q], side).start()
 
         @pl.when(t < ITERS - 1)
         def _():
@@ -349,10 +346,10 @@
             dma((2, n_sec)),
         ],
         compiler_params=pltpu.CompilerParams(
-            collective_id=0, has_side_effects=True, vmem_limit_bytes=48 * 1024 * 1024
+            collective_id=0, has_side_effects=True
         ),
         cost_estimate=pl.CostEstimate(flops=2 * n**3 * 4 * 200, bytes_accessed=4 * n * n * 60, transcendentals=0),
-    )(theta_in, left_env, site_maps, right_env, mpo_mask, ranks)
+    )(theta_in, left_env, site_maps, right_env, mpo_mask.T, ranks)
 
 
 def solution(mesh):

time: 50.6 us -> 44.2 us (0.87)
  local copies, waits for them, and re-layouts: 7.08 us -> 3.14 us
  Pallas kernels: 42.7 us -> 40.3 us
    unnamed x13 -> x2, local copies, waits for them, and re-layouts: 7.08 us -> 3.14 us
    pallas_call x1, Pallas kernels: 42.7 us -> 40.3 us  [per_device(): pl.pallas_call(functools.partial(kernel, n_seg, n_sec, groups), out_shape...]
where the time goes in v2:
time: 44.2 us; the launch traced here: 44 us
  Pallas kernels  40.3 us (91%)
  local copies, waits for them, and re-layouts  3.14 us (7%)
  between operations  0.64 us (1%)
    pallas_call x1, Pallas kernels, per_device(): pl.pallas_call(functools.partial(kernel, n_seg, n_sec, groups), out_shape...  40.3 us
    unnamed x2, local copies, waits for them, and re-layouts  3.14 us

profile of v2, /device:TPU:0, one launch (start us, length us, event | category | flops | bytes accessed | tf_op | source)
XLA Modules:
  0.0 44.0 jit_solution(2524187259382194228)
XLA Ops:
  0.6 40.3 %shard_map.77 = (f32[1,2,128,128]{3,2,1,0:T(8,128)}, f32[1,2,128,128]{3,2,1,0:T(8,128)}) custom-call(f32[1,2,128,128]{3,2,1,0:T(8,128)} %theta.1, f32[9,2,128,128]{3,2,1,0:T(8,128)} %left.1, f32[1,2,128,128]{3,2,1,0:T(8,128)} %maps.1, f32[1,9,2,128,128]{4,3,2,1,0:T(8,128)} %right.1, s32[2,9]{1,0:T(2,128)} %bitcast.1, s32[1,2]{1,0:T(1,128)} %ranks.1), custom_call_target="tpu_custom_call" | custom-call | flops 3355443200 | bytes 3932160 | tf_op jit(solution)/shard_map/pallas_call | solution.py:322
  40.9 1.6 %copy.10 = f32[1,2,128,128]{3,2,1,0:T(8,128)} copy(f32[1,2,128,128]{3,2,1,0:T(8,128)} %get-tuple-element.4) | data formatting | bytes 262144
  42.5 1.6 %copy.11 = f32[1,2,128,128]{3,2,1,0:T(8,128)} copy(f32[1,2,128,128]{3,2,1,0:T(8,128)} %get-tuple-element.5) | data formatting | bytes 262144

commit v3 on v2

--- a/solution.py
+++ b/solution.py
@@ -44,7 +44,7 @@
 def kernel(
     n_seg, n_sec, groups, theta, left, maps, right, mask, ranks, theta_out, density,
     lf, rt, mp, amat, rhalo, vh, vs, l2, r2, red,
-    local_sem, m_send, m_recv, r_send, r_recv, v_send, v_recv, s_send, s_recv,
+    local_sem, m_send, m_recv, m_pass, r_send, r_recv, v_send, v_recv, s_send, s_recv,
 ):
     seg, sec = lax.axis_index("seg"), lax.axis_index("sec")
     blocks, n = theta.shape[1], theta.shape[2]
@@ -84,6 +84,16 @@
             device_id={"seg": j}, device_id_type=MESH,
         )
 
+    def m_relay(j):
+        other = seg + 1 - 2 * lax.rem(seg, 2)
+        return pltpu.make_async_remote_copy(
+            src_ref=mp.at[j], dst_ref=mp.at[j], send_sem=m_pass.at[j], recv_sem=m_recv.at[j],
+            device_id={"seg": other}, device_id_type=MESH,
+        )
+
+    def m_direct(j):
+        return (j < seg) & (lax.rem(seg + j, 2) == 0)
+
     def v_copy(t, source, side):
         other = sec - 1 if side == 0 else sec + 1
         return pltpu.make_async_remote_copy(
@@ -133,8 +143,12 @@
             recv_sem=s_recv.at[stage, other], device_id={"sec": other}, device_id_type=MESH,
         )
 
-    for d in range(1, n_seg):
-        @pl.when(seg + d < n_seg)
+    def m_goes(d):
+        return lax.rem(seg, 2) == 0 if d == 1 else seg + d < n_seg
+
+    m_ways = [1] + list(range(2, n_seg, 2))
+    for d in reversed(m_ways):
+        @pl.when(m_goes(d))
         def _():
             m_copy(d).start()
 
@@ -163,6 +177,12 @@
                 for w in groups[d]:
                     r2[q, row[w] : row[w] + n, :] = wide(rt[w, q + d])
     loads[2].wait()
+
+    for j in range(n_seg - 2):
+        @pl.when(m_direct(j))
+        def _():
+            m_arrival(j).wait_recv()
+            m_relay(j).start()
 
     @pl.when(seg == 0)
     def _():
@@ -172,9 +192,12 @@
             amat[q] = (here == across).astype(F32)
 
     for j in range(n_seg - 1):
+        @pl.when((j < seg) & jnp.logical_not(m_direct(j)))
+        def _():
+            m_arrival(j).wait_recv()
+
         @pl.when(j < seg)
         def _():
-            m_arrival(j).wait_recv()
             for q in range(blocks):
                 if j == 0:
                     amat[q] = mp[0, q]
@@ -291,10 +314,14 @@
         theta_out[0, q] = theta_out[0, q] * s34
         density[0, q] = density[0, q] * (s34 * s34 / n)
 
-    for d in range(1, n_seg):
-        @pl.when(seg + d < n_seg)
+    for d in m_ways:
+        @pl.when(m_goes(d))
         def _():
             m_copy(d).wait_send()
+    for j in range(n_seg - 2):
+        @pl.when(m_direct(j))
+        def _():
+            m_relay(j).wait_send()
     for side, there in ((0, has_low), (1, has_high)):
         q = 0 if side == 0 else blocks - 1
         @pl.when(there)
@@ -314,7 +341,7 @@
     groups = {d: [w for w in range(terms) if w % 3 - 1 == d] for d in (-1, 0, 1)}
     most = max(len(g) for g in groups.values())
     block = (n, n)
-    anywhere = pl.BlockSpec(memory_space=pl.ANY)
+    anywhere = pl.BlockSpec(memory_space=pltpu.HBM)
     scalars = pl.BlockSpec(memory_space=pltpu.SMEM)
     vmem = pl.BlockSpec(memory_space=pltpu.VMEM)
     out = jax.ShapeDtypeStruct(theta_in.shape, F32)
@@ -338,6 +365,7 @@
             dma((3,)),
             dma((n_seg,)),
             dma((n_seg,)),
+            dma((n_seg,)),
             dma((2, most)),
             dma((2, most)),
             dma((ITERS, 2)),
@@ -346,7 +374,7 @@
             dma((2, n_sec)),
         ],
         compiler_params=pltpu.CompilerParams(
-            collective_id=0, has_side_effects=True
+            collective_id=0, has_side_effects=True, vmem_limit_bytes=40 * 1024 * 1024
         ),
         cost_estimate=pl.CostEstimate(flops=2 * n**3 * 4 * 200, bytes_accessed=4 * n * n * 60, transcendentals=0),
     )(theta_in, left_env, site_maps, right_env, mpo_mask.T, ranks)

time: 44.2 us -> 47.8 us (1.081)
  local copies, waits for them, and re-layouts: 3.14 us -> 6.99 us
    unnamed x2 -> x14, local copies, waits for them, and re-layouts: 3.14 us -> 6.99 us
where the time goes in v3:
time: 47.8 us; the launch traced here: 47.5 us
  Pallas kernels  39.9 us (83%)
  local copies, waits for them, and re-layouts  6.99 us (15%)
  between operations  0.65 us (1%)
    pallas_call x1, Pallas kernels, per_device(): pl.pallas_call(functools.partial(kernel, n_seg, n_sec, groups), out_shape...  39.9 us
    unnamed x14, local copies, waits for them, and re-layouts  6.99 us

profile of v3, /device:TPU:0, one launch (start us, length us, event | category | flops | bytes accessed | tf_op | source)
XLA Modules:
  0.0 47.5 jit_solution(6203929929374547702)
XLA Ops:
  0.6 0.0 copy-start
  0.6 1.3 %copy-done = f32[9,2,128,128]{3,2,1,0:T(8,128)S(1)} copy-done((f32[9,2,128,128]{3,2,1,0:T(8,128)S(1)}, f32[9,2,128,128]{3,2,1,0:T(8,128)}, u32[]{:S(2)}) %copy-start) | copy-done | bytes 1179672
  1.9 0.0 copy-start.1
  1.9 1.3 %copy-done.1 = f32[1,9,2,128,128]{4,3,2,1,0:T(8,128)S(1)} copy-done((f32[1,9,2,128,128]{4,3,2,1,0:T(8,128)S(1)}, f32[1,9,2,128,128]{4,3,2,1,0:T(8,128)}, u32[]{:S(2)}) %copy-start.1) | copy-done | bytes 1179672
  3.2 0.0 copy-start.2
  3.2 0.9 %copy-done.2 = f32[1,2,128,128]{3,2,1,0:T(8,128)S(1)} copy-done((f32[1,2,128,128]{3,2,1,0:T(8,128)S(1)}, f32[1,2,128,128]{3,2,1,0:T(8,128)}, u32[]{:S(2)}) %copy-start.2) | copy-done | bytes 131096
  4.1 0.0 copy-start.3
  4.1 0.9 %copy-done.3 = f32[1,2,128,128]{3,2,1,0:T(8,128)S(1)} copy-done((f32[1,2,128,128]{3,2,1,0:T(8,128)S(1)}, f32[1,2,128,128]{3,2,1,0:T(8,128)}, u32[]{:S(2)}) %copy-start.3) | copy-done | bytes 131096
  5.0 0.0 copy-start.4
  5.0 0.7 %copy-done.4 = s32[9,2]{0,1:T(2,128)S(1)} copy-done((s32[9,2]{0,1:T(2,128)S(1)}, s32[9,2]{0,1:T(2,128)}, u32[]{:S(2)}) %copy-start.4) | copy-done | bytes 96
  5.7 0.0 copy-start.5
  5.7 0.7 %copy-done.5 = s32[1,2]{1,0:T(1,128)S(1)} copy-done((s32[1,2]{1,0:T(1,128)S(1)}, s32[1,2]{1,0:T(1,128)}, u32[]{:S(2)}) %copy-start.5) | copy-done | bytes 32
  6.3 39.9 %shard_map.77 = (f32[1,2,128,128]{3,2,1,0:T(8,128)S(1)}, f32[1,2,128,128]{3,2,1,0:T(8,128)S(1)}) custom-call(f32[1,2,128,128]{3,2,1,0:T(8,128)S(1)} %copy-done.2, f32[9,2,128,128]{3,2,1,0:T(8,128)S(1)} %copy-done, f32[1,2,128,128]{3,2,1,0:T(8,128)S(1)} %copy-done.3, f32[1,9,2,128,128]{4,3,2,1,0:T(8,128)S(1)} %copy-done.1, s32[2,9]{1,0:T(2,128)S(1)} %bitcast.1, ...), custom_call_target="tpu_custom_call" | custom-call | flops 3355443200 | bytes 3932160 | tf_op jit(solution)/shard_map/pallas_call | solution.py:349
  46.2 0.7 %copy.10 = f32[1,2,128,128]{3,2,1,0:T(8,128)} copy(f32[1,2,128,128]{3,2,1,0:T(8,128)S(1)} %get-tuple-element.4) | data formatting | bytes 262144
  46.9 0.7 %copy.11 = f32[1,2,128,128]{3,2,1,0:T(8,128)} copy(f32[1,2,128,128]{3,2,1,0:T(8,128)S(1)} %get-tuple-element.5) | data formatting | bytes 262144
Async XLA Ops:
  0.6 1.3 %copy-start = (f32[9,2,128,128]{3,2,1,0:T(8,128)S(1)}, f32[9,2,128,128]{3,2,1,0:T(8,128)}, u32[]{:S(2)}) copy-start(f32[9,2,128,128]{3,2,1,0:T(8,128)} %left.1) | copy-start | bytes 3538948
  1.9 1.3 %copy-start.1 = (f32[1,9,2,128,128]{4,3,2,1,0:T(8,128)S(1)}, f32[1,9,2,128,128]{4,3,2,1,0:T(8,128)}, u32[]{:S(2)}) copy-start(f32[1,9,2,128,128]{4,3,2,1,0:T(8,128)} %right.1) | copy-start | bytes 3538948
  3.2 0.9 %copy-start.2 = (f32[1,2,128,128]{3,2,1,0:T(8,128)S(1)}, f32[1,2,128,128]{3,2,1,0:T(8,128)}, u32[]{:S(2)}) copy-start(f32[1,2,128,128]{3,2,1,0:T(8,128)} %theta.1) | copy-start | bytes 393220
  4.1 0.9 %copy-start.3 = (f32[1,2,128,128]{3,2,1,0:T(8,128)S(1)}, f32[1,2,128,128]{3,2,1,0:T(8,128)}, u32[]{:S(2)}) copy-start(f32[1,2,128,128]{3,2,1,0:T(8,128)} %maps.1) | copy-start | bytes 393220
  5.0 0.7 %copy-start.4 = (s32[9,2]{0,1:T(2,128)S(1)}, s32[9,2]{0,1:T(2,128)}, u32[]{:S(2)}) copy-start(s32[9,2]{0,1:T(2,128)} %param.10) | copy-start | bytes 220
  5.7 0.7 %copy-start.5 = (s32[1,2]{1,0:T(1,128)S(1)}, s32[1,2]{1,0:T(1,128)}, u32[]{:S(2)}) copy-start(s32[1,2]{1,0:T(1,128)} %ranks.1) | copy-start | bytes 28

commit v4 on v3

--- a/solution.py
+++ b/solution.py
@@ -336,17 +336,28 @@
             s_copy(stage, d).wait_send()
 
 
+def place(theta, density, theta_out, density_out, sem):
+    copies = [
+        pltpu.make_async_copy(theta, theta_out, sem.at[0]),
+        pltpu.make_async_copy(density, density_out, sem.at[1]),
+    ]
+    for copy in copies:
+        copy.start()
+    for copy in copies:
+        copy.wait()
+
+
 def per_device(n_seg, n_sec, theta_in, left_env, site_maps, right_env, mpo_mask, ranks):
     terms, blocks, n, _ = left_env.shape
     groups = {d: [w for w in range(terms) if w % 3 - 1 == d] for d in (-1, 0, 1)}
     most = max(len(g) for g in groups.values())
     block = (n, n)
-    anywhere = pl.BlockSpec(memory_space=pltpu.HBM)
+    anywhere = pl.BlockSpec(memory_space=pl.ANY)
     scalars = pl.BlockSpec(memory_space=pltpu.SMEM)
     vmem = pl.BlockSpec(memory_space=pltpu.VMEM)
     out = jax.ShapeDtypeStruct(theta_in.shape, F32)
     dma = pltpu.SemaphoreType.DMA
-    return pl.pallas_call(
+    results = pl.pallas_call(
         functools.partial(kernel, n_seg, n_sec, groups),
         out_shape=(out, out),
         in_specs=[anywhere, anywhere, anywhere, anywhere, scalars, scalars],
@@ -374,10 +385,17 @@
             dma((2, n_sec)),
         ],
         compiler_params=pltpu.CompilerParams(
-            collective_id=0, has_side_effects=True, vmem_limit_bytes=40 * 1024 * 1024
+            collective_id=0, has_side_effects=True
         ),
         cost_estimate=pl.CostEstimate(flops=2 * n**3 * 4 * 200, bytes_accessed=4 * n * n * 60, transcendentals=0),
     )(theta_in, left_env, site_maps, right_env, mpo_mask.T, ranks)
+    return pl.pallas_call(
+        place,
+        out_shape=(out, out),
+        in_specs=[anywhere, anywhere],
+        out_specs=(anywhere, anywhere),
+        scratch_shapes=[dma((2,))],
+    )(*results)
 
 
 def solution(mesh):

time: 47.8 us -> 50.2 us (1.050)
  Pallas kernels: 39.9 us -> 49.4 us
  local copies, waits for them, and re-layouts: 6.99 us -> 0 us
    pallas_call x0 -> x1, Pallas kernels: none -> 9.06 us  [per_device(): pl.pallas_call(place, out_shape=(out, out), in_specs=[anywhere, anywhere]...]
    unnamed x14 -> x0, local copies, waits for them, and re-layouts: 6.99 us -> none
where the time goes in v4:
time: 50.2 us; the launch traced here: 50 us
  Pallas kernels  49.4 us (98%)
  between operations  0.64 us (1%)
    pallas_call x1, Pallas kernels, per_device(): pl.pallas_call(functools.partial(kernel, n_seg, n_sec, groups), out_shape...  40.3 us
    pallas_call x1, Pallas kernels, per_device(): pl.pallas_call(place, out_shape=(out, out), in_specs=[anywhere, anywhere]...  9.06 us

profile of v4, /device:TPU:0, one launch (start us, length us, event | category | flops | bytes accessed | tf_op | source)
XLA Modules:
  0.0 50.0 jit_solution(12214541602552576465)
XLA Ops:
  0.6 40.3 %shard_map.77 = (f32[1,2,128,128]{3,2,1,0:T(8,128)}, f32[1,2,128,128]{3,2,1,0:T(8,128)}) custom-call(f32[1,2,128,128]{3,2,1,0:T(8,128)} %theta.1, f32[9,2,128,128]{3,2,1,0:T(8,128)} %left.1, f32[1,2,128,128]{3,2,1,0:T(8,128)} %maps.1, f32[1,9,2,128,128]{4,3,2,1,0:T(8,128)} %right.1, s32[2,9]{1,0:T(2,128)} %bitcast.1, s32[1,2]{1,0:T(1,128)} %ranks.1), custom_call_target="tpu_custom_call" | custom-call | flops 3355443200 | bytes 3932160 | tf_op jit(solution)/shard_map/pallas_call | solution.py:360
  40.9 9.1 %shard_map.78 = (f32[1,2,128,128]{3,2,1,0:T(8,128)}, f32[1,2,128,128]{3,2,1,0:T(8,128)}) custom-call(f32[1,2,128,128]{3,2,1,0:T(8,128)} %get-tuple-element.4.theta, f32[1,2,128,128]{3,2,1,0:T(8,128)} %get-tuple-element.5.density), custom_call_target="tpu_custom_call" | custom-call | tf_op jit(solution)/shard_map/pallas_call | solution.py:392

commit v5 on v4

--- a/solution.py
+++ b/solution.py
@@ -336,14 +336,16 @@
             s_copy(stage, d).wait_send()
 
 
-def place(theta, density, theta_out, density_out, sem):
-    copies = [
-        pltpu.make_async_copy(theta, theta_out, sem.at[0]),
-        pltpu.make_async_copy(density, density_out, sem.at[1]),
-    ]
-    for copy in copies:
+def place(theta, density, theta_out, density_out, held, sem):
+    arrays = ((theta, theta_out), (density, density_out))
+    arrivals = [pltpu.make_async_copy(a, held.at[i], sem.at[0, i]) for i, (a, _) in enumerate(arrays)]
+    departures = [pltpu.make_async_copy(held.at[i], b, sem.at[1, i]) for i, (_, b) in enumerate(arrays)]
+    for copy in arrivals:
         copy.start()
-    for copy in copies:
+    for arrival, departure in zip(arrivals, departures):
+        arrival.wait()
+        departure.start()
+    for copy in departures:
         copy.wait()
 
 
@@ -394,7 +396,7 @@
         out_shape=(out, out),
         in_specs=[anywhere, anywhere],
         out_specs=(anywhere, anywhere),
-        scratch_shapes=[dma((2,))],
+        scratch_shapes=[pltpu.VMEM((2,) + theta_in.shape, F32), dma((2, 2))],
     )(*results)
 
 

time: 50.2 us -> 42.7 us (0.85)
  Pallas kernels: 49.4 us -> 41.9 us
    pallas_call x1, Pallas kernels: 9.06 us -> 1.66 us  [per_device(): pl.pallas_call(place, out_shape=(out, out), in_specs=[anywhere, anywhere]...]
where the time goes in v5:
time: 42.7 us; the launch traced here: 42.6 us
  Pallas kernels  41.9 us (98%)
  between operations  0.64 us (1%)
    pallas_call x1, Pallas kernels, per_device(): pl.pallas_call(functools.partial(kernel, n_seg, n_sec, groups), out_shape...  40.3 us
    pallas_call x1, Pallas kernels, per_device(): pl.pallas_call(place, out_shape=(out, out), in_specs=[anywhere, anywhere]...  1.66 us

profile of v5, /device:TPU:0, one launch (start us, length us, event | category | flops | bytes accessed | tf_op | source)
XLA Modules:
  0.0 42.6 jit_solution(4022830298765753537)
XLA Ops:
  0.6 40.3 %shard_map.77 = (f32[1,2,128,128]{3,2,1,0:T(8,128)}, f32[1,2,128,128]{3,2,1,0:T(8,128)}) custom-call(f32[1,2,128,128]{3,2,1,0:T(8,128)} %theta.1, f32[9,2,128,128]{3,2,1,0:T(8,128)} %left.1, f32[1,2,128,128]{3,2,1,0:T(8,128)} %maps.1, f32[1,9,2,128,128]{4,3,2,1,0:T(8,128)} %right.1, s32[2,9]{1,0:T(2,128)} %bitcast.1, s32[1,2]{1,0:T(1,128)} %ranks.1), custom_call_target="tpu_custom_call" | custom-call | flops 3355443200 | bytes 3932160 | tf_op jit(solution)/shard_map/pallas_call | solution.py:362
  40.9 1.7 %shard_map.78 = (f32[1,2,128,128]{3,2,1,0:T(8,128)}, f32[1,2,128,128]{3,2,1,0:T(8,128)}) custom-call(f32[1,2,128,128]{3,2,1,0:T(8,128)} %get-tuple-element.4.theta, f32[1,2,128,128]{3,2,1,0:T(8,128)} %get-tuple-element.5.density), custom_call_target="tpu_custom_call" | custom-call | tf_op jit(solution)/shard_map/pallas_call | solution.py:394

commit v6 on v5

--- a/solution.py
+++ b/solution.py
@@ -43,7 +43,7 @@
 
 def kernel(
     n_seg, n_sec, groups, theta, left, maps, right, mask, ranks, theta_out, density,
-    lf, rt, mp, amat, rhalo, vh, vs, l2, r2, red,
+    lf, rt, mp, amat, rhalo, vh, vs, l2, r2, red, scale,
     local_sem, m_send, m_recv, m_pass, r_send, r_recv, v_send, v_recv, s_send, s_recv,
 ):
     seg, sec = lax.axis_index("seg"), lax.axis_index("sec")
@@ -221,6 +221,16 @@
         y = halves(dot(x, r2[q, start[d] : start[d] + size, :]))
         return y[:n] + y[n:]
 
+    cells = n_sec * blocks * n * n
+
+    def whole(stage):
+        total = red[stage, 0]
+        for other in range(1, n_sec):
+            total = total + red[stage, other]
+        first = jnp.sum(total[0], keepdims=True)
+        second = jnp.sum(total[1], keepdims=True)
+        return first / cells, second / cells
+
     def step(t, _):
         own = [twice(vs[t, q]) for q in range(blocks)]
         image = []
@@ -232,6 +242,14 @@
                     total = y if total is None else total + y
             vs[t + 1, q] = total
 
+        @pl.when(t == ITERS - 1)
+        def _():
+            for d in range(1, n_sec):
+                s_arrival(0, d).wait_recv()
+            m1, m2 = whole(0)
+            s1 = lax.rsqrt(m1 + EPS)
+            scale[...] = jnp.broadcast_to(s1 * lax.rsqrt(s1 * s1 * m2 + EPS), scale.shape)
+
         sides = ((0, has_low, 0, -1), (1, has_high, blocks - 1, 1))
 
         @pl.when(t == 0)
@@ -275,21 +293,7 @@
 
     lax.fori_loop(0, ITERS, step, 0)
 
-    cells = n_sec * blocks * n * n
-
-    def whole(stage):
-        total = red[stage, 0]
-        for other in range(1, n_sec):
-            total = total + red[stage, other]
-        first = jnp.sum(total[0], keepdims=True)
-        second = jnp.sum(total[1], keepdims=True)
-        return first / cells, second / cells
-
-    for d in range(1, n_sec):
-        s_arrival(0, d).wait_recv()
-    m1, m2 = whole(0)
-    s1 = lax.rsqrt(m1 + EPS)
-    s12 = s1 * lax.rsqrt(s1 * s1 * m2 + EPS)
+    s12 = scale[0:1, :]
     last = [vs[ITERS, q] * s12 for q in range(blocks)]
     total = squares(last[0])
     for q in range(1, blocks):
@@ -375,6 +379,7 @@
             pltpu.VMEM((blocks, terms * n, 2 * n), BF16),
             pltpu.VMEM((blocks, terms * n, 2 * n), BF16),
             pltpu.VMEM((2, n_sec, 2, 8, n), F32),
+            pltpu.VMEM((8, n), F32),
             dma((3,)),
             dma((n_seg,)),
             dma((n_seg,)),

time: 42.7 us -> 42.5 us (level)
  no operation moved by 1% of the time
where the time goes in v6:
time: 42.5 us; the launch traced here: 42.3 us
  Pallas kernels  41.7 us (98%)
  between operations  0.64 us (2%)
    pallas_call x1, Pallas kernels, per_device(): pl.pallas_call(functools.partial(kernel, n_seg, n_sec, groups), out_shape...  40 us
    pallas_call x1, Pallas kernels, per_device(): pl.pallas_call(place, out_shape=(out, out), in_specs=[anywhere, anywhere]...  1.66 us

profile of v6, /device:TPU:0, one launch (start us, length us, event | category | flops | bytes accessed | tf_op | source)
XLA Modules:
  0.0 42.3 jit_solution(7102847996175419780)
XLA Ops:
  0.6 40.0 %shard_map.77 = (f32[1,2,128,128]{3,2,1,0:T(8,128)}, f32[1,2,128,128]{3,2,1,0:T(8,128)}) custom-call(f32[1,2,128,128]{3,2,1,0:T(8,128)} %theta.1, f32[9,2,128,128]{3,2,1,0:T(8,128)} %left.1, f32[1,2,128,128]{3,2,1,0:T(8,128)} %maps.1, f32[1,9,2,128,128]{4,3,2,1,0:T(8,128)} %right.1, s32[2,9]{1,0:T(2,128)} %bitcast.1, s32[1,2]{1,0:T(1,128)} %ranks.1), custom_call_target="tpu_custom_call" | custom-call | flops 3355443200 | bytes 3932160 | tf_op jit(solution)/shard_map/pallas_call | solution.py:366
  40.7 1.7 %shard_map.78 = (f32[1,2,128,128]{3,2,1,0:T(8,128)}, f32[1,2,128,128]{3,2,1,0:T(8,128)}) custom-call(f32[1,2,128,128]{3,2,1,0:T(8,128)} %get-tuple-element.4.theta, f32[1,2,128,128]{3,2,1,0:T(8,128)} %get-tuple-element.5.density), custom_call_target="tpu_custom_call" | custom-call | tf_op jit(solution)/shard_map/pallas_call | solution.py:399

commit v7 on v6

--- a/solution.py
+++ b/solution.py
@@ -143,6 +143,20 @@
             recv_sem=s_recv.at[stage, other], device_id={"sec": other}, device_id_type=MESH,
         )
 
+    for side, there in ((0, has_low), (1, has_high)):
+        q = 0 if side == 0 else blocks - 1
+        @pl.when(there)
+        def _():
+            v_copy(0, theta.at[0, q], side).start()
+            for copy in r_copies(side):
+                copy.start()
+
+        @pl.when(jnp.logical_not(there))
+        def _():
+            rhalo[side] = jnp.zeros_like(rhalo[side])
+            for t in range(ITERS):
+                vh[t, side] = jnp.zeros_like(vh[t, side])
+
     def m_goes(d):
         return lax.rem(seg, 2) == 0 if d == 1 else seg + d < n_seg
 
@@ -151,20 +165,6 @@
         @pl.when(m_goes(d))
         def _():
             m_copy(d).start()
-
-    for side, there in ((0, has_low), (1, has_high)):
-        q = 0 if side == 0 else blocks - 1
-        @pl.when(there)
-        def _():
-            v_copy(0, theta.at[0, q], side).start()
-            for copy in r_copies(side):
-                copy.start()
-
-        @pl.when(jnp.logical_not(there))
-        def _():
-            rhalo[side] = jnp.zeros_like(rhalo[side])
-            for t in range(ITERS):
-                vh[t, side] = jnp.zeros_like(vh[t, side])
 
     loads[0].wait()
     for q in range(blocks):

time: 42.5 us -> 42.5 us (level)
  no operation moved by 1% of the time
where the time goes in v7:
time: 42.5 us; the launch traced here: 42.3 us
  Pallas kernels  41.7 us (98%)
  between operations  0.64 us (2%)
    pallas_call x1, Pallas kernels, per_device(): pl.pallas_call(functools.partial(kernel, n_seg, n_sec, groups), out_shape...  40 us
    pallas_call x1, Pallas kernels, per_device(): pl.pallas_call(place, out_shape=(out, out), in_specs=[anywhere, anywhere]...  1.66 us

profile of v7, /device:TPU:0, one launch (start us, length us, event | category | flops | bytes accessed | tf_op | source)
XLA Modules:
  0.0 42.3 jit_solution(5043097972352824049)
XLA Ops:
  0.6 40.0 %shard_map.77 = (f32[1,2,128,128]{3,2,1,0:T(8,128)}, f32[1,2,128,128]{3,2,1,0:T(8,128)}) custom-call(f32[1,2,128,128]{3,2,1,0:T(8,128)} %theta.1, f32[9,2,128,128]{3,2,1,0:T(8,128)} %left.1, f32[1,2,128,128]{3,2,1,0:T(8,128)} %maps.1, f32[1,9,2,128,128]{4,3,2,1,0:T(8,128)} %right.1, s32[2,9]{1,0:T(2,128)} %bitcast.1, s32[1,2]{1,0:T(1,128)} %ranks.1), custom_call_target="tpu_custom_call" | custom-call | flops 3355443200 | bytes 3932160 | tf_op jit(solution)/shard_map/pallas_call | solution.py:366
  40.7 1.7 %shard_map.78 = (f32[1,2,128,128]{3,2,1,0:T(8,128)}, f32[1,2,128,128]{3,2,1,0:T(8,128)}) custom-call(f32[1,2,128,128]{3,2,1,0:T(8,128)} %get-tuple-element.4.theta, f32[1,2,128,128]{3,2,1,0:T(8,128)} %get-tuple-element.5.density), custom_call_target="tpu_custom_call" | custom-call | tf_op jit(solution)/shard_map/pallas_call | solution.py:399
